TPU v7x, 256 devices: a whole 4x4x8 slice. The times are simulated.
256 devices in a mesh: row: 64 (over y, z, core), col: 4 (over x).
Axes of the slice: x: 4, y: 4, z: 8, core: 2. Of those that a mesh axis runs over, the one named last changes fastest.
Arguments:
- entity_feats: bfloat16 [65536, 256], P(('col', 'row')), may hold values from -6 to 6
- class_map: int32 [65536], P(('col', 'row')), may hold values from 0 to 127, as said below
- tile_values: bfloat16 [8192, 128, 128], P(('row', 'col')), may hold values from -0.09375 to 0.09375
- tile_rows: int32 [8192], P(('row', 'col')), may hold values from 0 to 3
- tile_column_index: int32 [8192], P(('row', 'col')), may hold values from 0 to 63
- tile_rels: int32 [8192], P(('row', 'col')), may hold values from 0 to 499
- tile_counts: int32 [256], P(('row', 'col')), may hold values from 4 to 32, as said below
- coefficients: bfloat16 [500, 8], replicated, may hold values from -2 to 2
- bases: bfloat16 [8, 256, 256], replicated, may hold values from -0.375 to 0.375
- cotangent: bfloat16 [32768, 256], P(('row', 'col')), may hold values from -6 to 6
Outputs:
- layer_out: bfloat16 [32768, 256], P(('row', 'col'))
- grad_entities: float32 [65536, 256], P(('col', 'row'))
- grad_bases: float32 [8, 256, 256], replicated
- grad_coef: float32 [500, 8], replicated
Inputs may be any that keep to these rules, and one draw needn't show every extreme that they name: `class_map`: within every block of 256 entities, every class number 0 to 127 occurs at least once. `tile_counts`: tile slots of a device from its count onward are unused; some device has all 32 slots live in every draw.
All inputs are finite; a program needn't handle non-finite values.
Results may differ from a plain program's by a relative error of at most 0.006.
Values may be sent and summed in bfloat16 or wider, within the bound.
No kernel may reach another device: no remote copies, remote signals or barrier semaphores. Data moves between devices by JAX's collectives and lax.ppermute only.
A program may use at most 128 MiB of HBM per device.

v0:
```python
import jax
import jax.numpy as jnp
from jax import lax
from jax.sharding import PartitionSpec as P

TBLK = 32


def tile_weights(rel_block, row_block, live, coefficients, trows, relations):
    pick_rel = (rel_block[:, None] == jnp.arange(relations, dtype=jnp.int32)[None, :]).astype(
        jnp.bfloat16
    )
    coef_rows = jnp.dot(pick_rel, coefficients, preferred_element_type=jnp.float32)
    pick_row = (
        (row_block[:, None] == jnp.arange(trows, dtype=jnp.int32)[None, :]) & live[:, None]
    ).astype(jnp.float32)
    weights = (pick_row[:, :, None] * coef_rows[:, None, :]).astype(jnp.bfloat16)
    return (weights, pick_row)


def local(
    entity_feats,
    class_map,
    tile_values,
    tile_rows,
    tile_column_index,
    tile_rels,
    tile_counts,
    coefficients,
    bases,
    cotangent,
):
    n_row = lax.axis_size("row")
    n_col = lax.axis_size("col")
    node_dev = cotangent.shape[0]
    tile = tile_values.shape[1]
    nbases = bases.shape[0]
    width = bases.shape[1]
    relations = coefficients.shape[0]
    rblock = node_dev * n_col
    cblock = node_dev * n_row
    trows = rblock // tile
    tile_column_list = cblock // tile
    member = class_map[:, None] == jnp.arange(node_dev, dtype=jnp.int32)[None, :]
    member_bf = member.astype(jnp.bfloat16)
    sums = lax.dot_general(
        member_bf, entity_feats, (((0,), (0,)), ((), ())), preferred_element_type=jnp.float32
    )
    counts = jnp.sum(member.astype(jnp.float32), axis=0)
    class_feat = (sums / counts[:, None]).astype(jnp.bfloat16)
    sender_device = lax.all_gather(class_feat, "row", axis=0, tiled=True).reshape(
        tile_column_list, tile, width
    )
    stacked = bases.reshape(nbases * width, width)
    live_count = tile_counts[0]
    turns = (live_count + TBLK - 1) // TBLK

    def forward_turn(step, carry):
        sums_acc, msg_store = carry
        leading_entry = step * TBLK
        live = leading_entry + jnp.arange(TBLK, dtype=jnp.int32) < live_count
        selected_entries = jnp.take(sender_device, tile_column_index, axis=0)
        messages = jnp.einsum(
            "kij,kjh->kih", tile_values, selected_entries, preferred_element_type=jnp.float32
        ).astype(jnp.bfloat16)
        weights, pick_row = tile_weights(tile_rels, tile_rows, live, coefficients, trows, relations)
        sums_acc = sums_acc + jnp.einsum(
            "ktb,kih->tibh", weights, messages, preferred_element_type=jnp.float32
        )
        msg_store = messages
        return (sums_acc, msg_store)

    init_sums = jnp.zeros((trows, tile, nbases, width), jnp.float32)
    init_store = jnp.zeros((tile_values.shape[0], tile, width), jnp.bfloat16)
    sums_acc, msg_store = lax.fori_loop(0, turns, forward_turn, (init_sums, init_store))
    part = sums_acc.astype(jnp.bfloat16).reshape(rblock, nbases * width)
    out_part = jnp.dot(part, stacked, preferred_element_type=jnp.float32)
    layer_out = lax.psum_scatter(out_part, "col", scatter_dimension=0, tiled=True).astype(
        jnp.bfloat16
    )
    dout_rows = lax.all_gather(cotangent, "col", axis=0, tiled=True)
    grads_rows = lax.dot_general(
        dout_rows, stacked, (((1,), (1,)), ((), ())), preferred_element_type=jnp.float32
    ).astype(jnp.bfloat16)
    dv_part = lax.dot_general(
        part, dout_rows, (((0,), (0,)), ((), ())), preferred_element_type=jnp.float32
    )
    grads_tiles = grads_rows.reshape(trows, tile, nbases, width)

    def backward_turn(step, carry):
        dcoef_acc, dx_acc = carry
        leading_entry = step * TBLK
        live = leading_entry + jnp.arange(TBLK, dtype=jnp.int32) < live_count
        weights, pick_row = tile_weights(tile_rels, tile_rows, live, coefficients, trows, relations)
        gram = jnp.einsum(
            "kih,tibh->ktb", msg_store, grads_tiles, preferred_element_type=jnp.float32
        )
        per_tile = jnp.sum(gram * pick_row[:, :, None], axis=1)
        dcoef_acc = dcoef_acc + jax.ops.segment_sum(per_tile, tile_rels, num_segments=relations)
        mixed = jnp.einsum(
            "ktb,tibh->kih", weights, grads_tiles, preferred_element_type=jnp.float32
        ).astype(jnp.bfloat16)
        back = jnp.einsum("kij,kih->kjh", tile_values, mixed, preferred_element_type=jnp.float32)
        dx_acc = dx_acc.at[tile_column_index].add(back)
        return (dcoef_acc, dx_acc)

    init_coef = jnp.zeros((relations, nbases), jnp.float32)
    init_dx = jnp.zeros((tile_column_list, tile, width), jnp.float32)
    dcoef_acc, dx_acc = lax.fori_loop(0, turns, backward_turn, (init_coef, init_dx))
    dx_all = dx_acc.reshape(cblock, width)
    dx_own = lax.psum_scatter(dx_all, "row", scatter_dimension=0, tiled=True)
    dv_sum, dcoef_sum = lax.psum((dv_part, dcoef_acc), ("row", "col"))
    scale = (node_dev * n_row * n_col) ** (-0.5)
    grad_bases = (dv_sum * scale).reshape(nbases, width, width)
    grad_coef = dcoef_sum * scale
    quotient = dx_own / counts[:, None]
    grad_entities = jnp.dot(member.astype(jnp.float32), quotient, precision=lax.Precision.HIGHEST)
    return (layer_out, grad_entities, grad_bases, grad_coef)


def solution(mesh):
    placed = (
        P(("col", "row"), None),
        P(("col", "row")),
        P(("row", "col"), None, None),
        P(("row", "col")),
        P(("row", "col")),
        P(("row", "col")),
        P(("row", "col")),
        P(),
        P(),
        P(("row", "col"), None),
    )
    return jax.shard_map(
        local,
        mesh=mesh,
        in_specs=placed,
        out_specs=(P(("row", "col"), None), P(("col", "row"), None), P(), P()),
        check_vma=False,
    )
```

profile of v0, /device:TPU:2, one launch (start us, length us, event | category | flops | bytes accessed | tf_op | source)
XLA Modules:
  0.0 570.0 jit_solution(12668102719578885372)
XLA Ops:
  7.2 0.9 convert_reduce_fusion
  8.1 1.8 fusion.22
  10.7 12.6 %all_gather.7 = bf16[512,256]{1,0:T(8,128)(2,1)S(1)} all-gather(bf16[128,256]{1,0:T(8,128)(2,1)} %param.23), channel_id=1, replica_groups=mesh['row'=64,'col'=4] {'col'}, dimensions={0}, use_global_device_ids=true | all-gather | bytes 327680 | tf_op jit(solution)/shard_map/all_gather | solution.py:81
  23.3 0.7 compare_select_fusion.1
  23.9 0.7 compare_and_fusion
  24.6 0.9 fusion.32
  25.5 67.9 %all-gather.2.cloned.1.call-done = bf16[8192,256]{1,0:T(8,128)(2,1)} async-done(((bf16[128,256]{1,0:T(8,128)(2,1)}), bf16[8192,256]{1,0:T(8,128)(2,1)}) %all-gather.2.cloned.1.call-update) | async-done | bytes 4194320 | tf_op jit(solution)/shard_map/all_gather | solution.py:51
  93.4 4.3 gather_fusion
  97.7 3.8 convert_bitcast_fusion
  101.4 3.4 copy.35
  104.8 1.6 broadcast_in_dim.33
  106.4 2.3 broadcast_in_dim.32
  108.7 6.6 %while.31 = (s32[]{:T(128)}, f32[4,128,8,256]{3,2,1,0:T(8,128)}, bf16[32,128,256]{2,0,1:T(8,128)(2,1)}, s32[]{:T(128)}, s32[32]{0:T(128)S(1)}, /*index=5*/s32[]{...) while((s32[]{:T(128)}, f32[4,128,8,256]{3,2,1,0:T(8,128)}, ...), condition=%wide.region_2.3_spmd, body=%wide.region_1.2_spmd.sunk | while | flops 68159936 | bytes 48236912 | solution.py:75
  108.7 0.7 add_compare_fusion.4
  109.4 1.3 copy.62
  110.7 1.6 copy-done.1
  112.3 1.1 bitcast_add_fusion.2
  113.4 1.9 copy-done.2
  115.3 2.4 convert_element_type.73
  117.7 0.7 copy.42
  118.4 1.3 copy-done.5
  119.8 2.1 fusion.37
  121.9 0.7 convolution_convert_fusion
  122.7 0.7 copy.43
  123.4 0.3 copy.36
  123.6 1.3 copy-done.7
  124.9 0.7 fusion.23
  125.6 0.9 copy-done.6
  126.5 1.5 fusion.36
  128.2 4.3 broadcast_in_dim.46
  132.4 22.2 %while.32 = (s32[]{:T(128)}, f32[500,8]{1,0:T(8,128)S(1)}, f32[64,128,256]{2,1,0:T(8,128)}, s32[]{:T(128)}, s32[32]{0:T(128)S(1)}, /*index=5*/s32[32]{0:T(128)S(...) while((s32[]{:T(128)}, f32[500,8]{1,0:T(8,128)S(1)}, ...), condition=%wide.region_8.9_spmd, body=%wide.region_4.8_spmd.sunk | while | flops 337646112 | bytes 36713844 | solution.py:109
  132.4 0.7 add_compare_fusion.5
  133.1 0.1 copy.50
  133.2 0.8 scatter_fusion
  134.1 0.7 bitcast_convert_fusion.2
  134.8 0.5 copy-done.4
  135.3 3.7 convolution_bitcast_fusion.2
  139.0 5.6 copy.51
  144.6 10.1 %scatter_fusion.1 = f32[64,128,256]{2,1,0:T(8,128)} fusion(f32[64,128,256]{2,1,0:T(8,128)} %get-tuple-element.645, s32[32]{0:T(128)S(1)} %fusion.66, f32[32,128,256]{2,1,0:T(8,128)} %copy.51), kind=kCustom, calls=%fused_computation.2.clone.1 | custom fusion | flops 1048576 | bytes 12583040 | tf_op jit(solution)/shard_map/while/body/scatter-add | solution.py:104
  154.7 0.1 copy.37
  154.8 75.1 %psum.15 = f32[500,8]{0,1:T(8,128)S(1)} all-reduce(f32[500,8]{0,1:T(8,128)S(1)} %copy.37), channel_id=1, replica_groups=mesh['row'=64,'col'=4] {'row','col'}, use_global_device_ids=true, to_apply=%region_11.12 | all-reduce | flops 4000 | bytes 32000 | tf_op jit(solution)/shard_map/psum | solution.py:112
  229.9 0.6 broadcast_multiply_fusion.1
  230.5 150.1 %all-reduce.2.cloned.1.call-done = f32[2048,256]{1,0:T(8,128)} async-done(((f32[2048,256]{1,0:T(8,128)}), f32[2048,256]{1,0:T(8,128)}) %all-reduce.2.cloned.1.call-update) | async-done | bytes 2097168 | tf_op jit(solution)/shard_map/psum | solution.py:112
  380.6 3.1 broadcast_multiply_fusion
  383.7 20.1 %reduce-scatter.3.cloned.1.call-done = f32[128,256]{1,0:T(8,128)} async-done(((f32[512,256]{1,0:T(8,128)}), f32[128,256]{1,0:T(8,128)}) %reduce-scatter.3.cloned.1.call-update) | async-done | bytes 131088 | tf_op jit(solution)/shard_map/reduce_scatter | solution.py:78
  403.8 1.5 convert_element_type.74
  405.3 156.1 %reduce-scatter.5.cloned.1.call-done = f32[128,256]{1,0:T(8,128)} async-done(((f32[8192,256]{1,0:T(8,128)}), f32[128,256]{1,0:T(8,128)}) %reduce-scatter.5.cloned.1.call-update) | async-done | bytes 131088 | tf_op jit(solution)/shard_map/reduce_scatter | solution.py:111
  561.5 2.0 fusion.27
  (32 shorter events, 0.3 us)
Async XLA Ops:
  7.2 114.7 %copy-start = (bf16[8,256,256]{2,1,0:T(8,128)(2,1)S(1)}, bf16[8,256,256]{2,1,0:T(8,128)(2,1)}, u32[]{:S(2)}) copy-start(bf16[8,256,256]{2,1,0:T(8,128)(2,1)} %param.22) | copy-start | bytes 3145732
  7.2 86.2 %all-gather.2.cloned.1.call-start = ((), (), s32[]{:S(2)}) async-start(), calls=%async_computation.2 | async-start | bytes 4259840 | tf_op jit(solution)/shard_map/all_gather | solution.py:51
  10.0 370.7 %all-reduce.2.cloned.1.call-start = ((), (), s32[]{:S(2)}) async-start(), calls=%async_computation.5 | async-start | bytes 4194304 | tf_op jit(solution)/shard_map/psum | solution.py:112
  93.4 4.3 copy-start.3
  106.4 2.3 copy-start.8
  109.4 2.9 copy-start.1
  113.4 1.9 copy-start.2
  118.4 1.3 copy-start.5
  121.9 282.0 %reduce-scatter.3.cloned.1.call-start = ((), (), s32[]{:S(2)}) async-start(), calls=%async_computation.3 | async-start | bytes 655360 | tf_op jit(solution)/shard_map/reduce_scatter | solution.py:78
  123.3 1.6 copy-start.7
  124.9 1.6 copy-start.6
  128.1 433.4 %reduce-scatter.5.cloned.1.call-start = ((), (), s32[]{:S(2)}) async-start(), calls=%async_computation.4 | async-start | bytes 8519680 | tf_op jit(solution)/shard_map/reduce_scatter | solution.py:111
  128.2 4.3 copy-start.9
  128.2 4.3 copy-start.11
  134.1 1.2 copy-start.4
  230.5 331.0 %copy-start.10 = (s32[256]{0:T(256)S(1)}, s32[256]{0:T(256)}, u32[]{:S(2)}) copy-start(s32[256]{0:T(256)} %param.15) | copy-start | bytes 3076
Sparse Core Ops, SparseCore 0:
  11.4 81.9 all-gather.1
  122.0 258.6 all-reduce.1
  383.2 20.6 reduce-scatter.2
  407.9 153.5 reduce-scatter.4
where the time goes:
time: 571 us; the launch traced here: 570 us
  waiting for transfers between devices  394 us (69%)
  blocking collectives  87.6 us (15%)
  local copies, waits for them, and re-layouts  32.2 us (6%)
  other arithmetic  22.1 us (4%)
  matrix products  18.9 us (3%)
  between operations  14.5 us (3%)
    reduce_scatter x1, waiting for transfers between devices, local(): dx_own = lax.psum_scatter(dx_all, 'row', scatter_dimension=0, tiled=True)  156 us
    psum x1, waiting for transfers between devices, local(): dv_sum, dcoef_sum = lax.psum((dv_part, dcoef_acc), ('row', 'col'))  150 us
    psum x1, blocking collectives, local(): dv_sum, dcoef_sum = lax.psum((dv_part, dcoef_acc), ('row', 'col'))  75.1 us
    all_gather x1, waiting for transfers between devices, local(): lax.all_gather(class_feat, 'row', axis=0, tiled=True)  67.9 us
    reduce_scatter x1, waiting for transfers between devices, local(): lax.psum_scatter(out_part, 'col', scatter_dimension=0, tiled=True)  20.1 us
    all_gather x1, blocking collectives, local(): dout_rows = lax.all_gather(cotangent, 'col', axis=0, tiled=True)  12.6 us
  transfers between devices with their start and end apart: 4, of which 4 were waited for; matrix products, arithmetic and copies ran while one was open for 7% of the time, Pallas kernels for 0%

commit v1 on v0

--- a/solution.py
+++ b/solution.py
@@ -4,6 +4,27 @@
 from jax.sharding import PartitionSpec as P
 
 TBLK = 32
+
+
+def joined_along(blocks, dim):
+    blocks = jnp.moveaxis(blocks, 0, dim)
+    shape = blocks.shape
+    return blocks.reshape(*shape[:dim], shape[dim] * shape[dim + 1], *shape[dim + 2 :])
+
+
+def grow_blocks(x, axis):
+    peers, index = (lax.axis_size(axis), lax.axis_index(axis))
+    blocks, apart = (x[None], 1)
+    while apart < peers:
+        other = lax.ppermute(blocks, axis, [(i, i ^ apart) for i in range(peers)])
+        low = index & apart == 0
+        blocks = jnp.concatenate([jnp.where(low, blocks, other), jnp.where(low, other, blocks)])
+        apart *= 2
+    return blocks
+
+
+def doubled_up(x, axis, dim):
+    return joined_along(grow_blocks(x, axis), dim)
 
 
 def tile_weights(rel_block, row_block, live, coefficients, trows, relations):
@@ -48,9 +69,7 @@
     )
     counts = jnp.sum(member.astype(jnp.float32), axis=0)
     class_feat = (sums / counts[:, None]).astype(jnp.bfloat16)
-    sender_device = lax.all_gather(class_feat, "row", axis=0, tiled=True).reshape(
-        tile_column_list, tile, width
-    )
+    sender_device = doubled_up(class_feat, "row", 0).reshape(tile_column_list, tile, width)
     stacked = bases.reshape(nbases * width, width)
     live_count = tile_counts[0]
     turns = (live_count + TBLK - 1) // TBLK

time: 571 us -> 451 us (0.79)
  waiting for transfers between devices: 394 us -> 247 us
  starting transfers between devices: 0.16 us -> 16.8 us
  other arithmetic: 22.1 us -> 28.5 us
    reduce_scatter x1, waiting for transfers between devices: 156 us -> 0.01 us  [local(): dx_own = lax.psum_scatter(dx_all, 'row', scatter_dimension=0, tiled=True)]
    ppermute x0 -> x6, waiting for transfers between devices: none -> 92.9 us  [grow_blocks(): other = lax.ppermute(blocks, axis, [(i, i ^ apart) for i in range(peers)])]
    all_gather x1 -> x0, waiting for transfers between devices: 67.9 us -> none  [local(): lax.all_gather(class_feat, 'row', axis=0, tiled=True)]
    reduce_scatter x1, waiting for transfers between devices: 20.1 us -> 0.01 us  [local(): lax.psum_scatter(out_part, 'col', scatter_dimension=0, tiled=True)]
    ppermute x0 -> x6, starting transfers between devices: none -> 16.5 us  [grow_blocks(): other = lax.ppermute(blocks, axis, [(i, i ^ apart) for i in range(peers)])]
  transfers between devices with their start and end apart: 4 -> 9, of which waited for: 4 -> 7; matrix products, arithmetic and copies ran while one was open for 7% -> 8% of each run, Pallas kernels for 0% -> 0%
where the time goes in v1:
time: 451 us; the launch traced here: 450 us
  waiting for transfers between devices  247 us (55%)
  blocking collectives  90.6 us (20%)
  local copies, waits for them, and re-layouts  32.7 us (7%)
  other arithmetic  28.5 us (6%)
  matrix products  17.6 us (4%)
  starting transfers between devices  16.8 us (4%)
  between operations  16.4 us (4%)
    psum x1, waiting for transfers between devices, local(): dv_sum, dcoef_sum = lax.psum((dv_part, dcoef_acc), ('row', 'col'))  154 us
    ppermute x6, waiting for transfers between devices, grow_blocks(): other = lax.ppermute(blocks, axis, [(i, i ^ apart) for i in range(peers)])  92.9 us
    psum x1, blocking collectives, local(): dv_sum, dcoef_sum = lax.psum((dv_part, dcoef_acc), ('row', 'col'))  78.3 us
    ppermute x6, starting transfers between devices, grow_blocks(): other = lax.ppermute(blocks, axis, [(i, i ^ apart) for i in range(peers)])  16.5 us
    all_gather x1, blocking collectives, local(): dout_rows = lax.all_gather(cotangent, 'col', axis=0, tiled=True)  12.3 us
    scatter-add x1, other arithmetic, backward_turn(): dx_acc = dx_acc.at[tile_column_index].add(back)  10.1 us
  transfers between devices with their start and end apart: 9, of which 7 were waited for; matrix products, arithmetic and copies ran while one was open for 8% of the time, Pallas kernels for 0%

profile of v1, /device:TPU:2, one launch (start us, length us, event | category | flops | bytes accessed | tf_op | source)
XLA Modules:
  0.0 450.0 jit_solution(7589730505519121256)
XLA Ops:
  8.1 0.9 convert_reduce_fusion
  8.9 1.2 fusion.23
  10.3 1.2 collective-permute-done
  11.5 2.0 collective-permute-start.1
  13.5 3.8 collective-permute-done.1
  17.4 3.4 collective-permute-start.2
  20.8 11.6 %collective-permute-done.2 = bf16[4,128,256]{2,1,0:T(8,128)(2,1)S(1)} collective-permute-done((bf16[4,128,256]{2,1,0:T(8,128)(2,1)S(1)}, bf16[4,128,256]{2,1,0:T(8,128)(2,1)S(1)}, u32[]{:S(2)}, u32[]{:S(2)}) %collective-permute-start.2) | collective-permute-done | bytes 262176 | tf_op jit(solution)/shard_map/ppermute | solution.py:19
  32.5 6.3 %collective-permute-start.3 = (bf16[8,128,256]{2,1,0:T(8,128)(2,1)S(1)}, bf16[8,128,256]{2,1,0:T(8,128)(2,1)S(1)}, u32[]{:S(2)}, u32[]{:S(2)}) collective-permute-start(bf16[8,128,256]{2,1,0:T(8,128)(2,1)S(1)} %pad_maximum_fusion.3), channel_id=1, source_target_pairs={{0,32},{4,36},{8,40},{12,44},{16,48},{20,52},{24,56},{28,60},{32,0... | collective-permute-start | bytes 1572872 | tf_op jit(solution)/shard_map/ppermute | solution.py:19
  38.8 23.0 %collective-permute-done.3 = bf16[8,128,256]{2,1,0:T(8,128)(2,1)S(1)} collective-permute-done((bf16[8,128,256]{2,1,0:T(8,128)(2,1)S(1)}, bf16[8,128,256]{2,1,0:T(8,128)(2,1)S(1)}, u32[]{:S(2)}, u32[]{:S(2)}) %collective-permute-start.3) | collective-permute-done | bytes 524320 | tf_op jit(solution)/shard_map/ppermute | solution.py:19
  61.8 0.8 copy-done.9
  62.8 1.6 collective-permute-start.4
  64.4 22.4 %collective-permute-done.4 = bf16[16,128,256]{2,1,0:T(8,128)(2,1)} collective-permute-done((bf16[16,128,256]{2,1,0:T(8,128)(2,1)S(1)}, bf16[16,128,256]{2,1,0:T(8,128)(2,1)}, u32[]{:S(2)}, u32[]{:S(2)}) %collective-permute-start.4) | collective-permute-done | bytes 1048608 | tf_op jit(solution)/shard_map/ppermute | solution.py:19
  86.8 1.7 broadcast_select_fusion.3
  88.5 1.5 pad_maximum_fusion.1
  90.0 3.2 collective-permute-start.5
  93.9 12.3 %all_gather.3 = bf16[512,256]{1,0:T(8,128)(2,1)S(1)} all-gather(bf16[128,256]{1,0:T(8,128)(2,1)S(1)} %copy-done.11), channel_id=1, replica_groups=mesh['row'=64,'col'=4] {'col'}, dimensions={0}, use_global_device_ids=true | all-gather | bytes 327680 | tf_op jit(solution)/shard_map/all_gather | solution.py:100
  106.5 30.8 %collective-permute-done.5 = bf16[32,128,256]{2,1,0:T(8,128)(2,1)} collective-permute-done((bf16[32,128,256]{2,1,0:T(8,128)(2,1)}, bf16[32,128,256]{2,1,0:T(8,128)(2,1)}, u32[]{:S(2)}, u32[]{:S(2)}) %collective-permute-start.5) | collective-permute-done | bytes 2097184 | tf_op jit(solution)/shard_map/ppermute | solution.py:19
  137.3 1.9 broadcast_select_fusion.1
  139.2 2.3 pad_maximum_fusion
  141.5 4.3 gather_fusion
  145.8 3.8 convert_bitcast_fusion
  149.5 3.4 copy.36
  153.0 1.6 broadcast_in_dim.35
  154.5 2.3 broadcast_in_dim.34
  156.9 6.7 %while.31 = (s32[]{:T(128)}, f32[4,128,8,256]{3,2,1,0:T(8,128)}, bf16[32,128,256]{2,0,1:T(8,128)(2,1)}, s32[]{:T(128)}, s32[32]{0:T(128)S(1)}, /*index=5*/s32[]{...) while((s32[]{:T(128)}, f32[4,128,8,256]{3,2,1,0:T(8,128)}, ...), condition=%wide.region_2.3_spmd, body=%wide.region_1.2_spmd.sunk | while | flops 68159936 | bytes 48236912 | solution.py:94
  157.5 1.3 copy.63
  158.9 1.6 copy-done.2
  160.5 1.1 bitcast_add_fusion.2
  161.6 2.0 copy-done.3
  163.5 2.4 convert_element_type.73
  166.6 1.3 copy-done.6
  167.9 2.1 fusion.38
  170.3 0.7 convolution_convert_fusion
  172.0 1.3 copy-done.8
  174.0 0.9 copy-done.7
  174.9 1.5 fusion.37
  176.6 4.3 broadcast_in_dim.57
  180.8 21.8 %while.32 = (s32[]{:T(128)}, f32[500,8]{1,0:T(8,128)S(1)}, f32[64,128,256]{2,1,0:T(8,128)}, s32[]{:T(128)}, s32[32]{0:T(128)S(1)}, /*index=5*/s32[32]{0:T(128)S(...) while((s32[]{:T(128)}, f32[500,8]{1,0:T(8,128)S(1)}, ...), condition=%wide.region_8.9_spmd, body=%wide.region_4.8_spmd.sunk | while | flops 337646112 | bytes 32519512 | solution.py:128
  181.6 0.8 scatter_fusion
  182.5 0.7 bitcast_convert_fusion.2
  183.2 3.7 convolution_bitcast_fusion.2
  186.9 5.7 %copy.52 = f32[32,128,256]{2,1,0:T(8,128)} copy(f32[32,128,256]{1,2,0:T(8,128)} %convolution_bitcast_fusion.2) | data formatting | bytes 8388608 | tf_op jit(solution)/shard_map/while/body/kij,kih->kjh/dot_general | solution.py:122
  192.5 10.1 %scatter_fusion.1 = f32[64,128,256]{2,1,0:T(8,128)} fusion(f32[64,128,256]{2,1,0:T(8,128)} %get-tuple-element.657, s32[32]{0:T(128)S(1)} %fusion.67, f32[32,128,256]{2,1,0:T(8,128)} %copy.52), kind=kCustom, calls=%fused_computation.2.clone.1 | custom fusion | flops 1048576 | bytes 12583040 | tf_op jit(solution)/shard_map/while/body/scatter-add | solution.py:123
  202.8 78.3 %psum.15 = f32[500,8]{0,1:T(8,128)S(1)} all-reduce(f32[500,8]{0,1:T(8,128)S(1)} %copy.38), channel_id=1, replica_groups=mesh['row'=64,'col'=4] {'row','col'}, use_global_device_ids=true, to_apply=%region_11.12 | all-reduce | flops 4000 | bytes 32000 | tf_op jit(solution)/shard_map/psum | solution.py:131
  281.7 154.3 %all-reduce.2.cloned.1.call-done = f32[2048,256]{1,0:T(8,128)} async-done(((f32[2048,256]{1,0:T(8,128)}), f32[2048,256]{1,0:T(8,128)}) %all-reduce.2.cloned.1.call-update) | async-done | bytes 2097168 | tf_op jit(solution)/shard_map/psum | solution.py:131
  436.0 3.1 broadcast_multiply_fusion
  439.1 1.5 convert_element_type.74
  440.6 2.0 fusion.28
  (63 shorter events, 5.6 us)
Async XLA Ops:
  8.0 162.3 %copy-start = (bf16[8,256,256]{2,1,0:T(8,128)(2,1)S(1)}, bf16[8,256,256]{2,1,0:T(8,128)(2,1)}, u32[]{:S(2)}) copy-start(bf16[8,256,256]{2,1,0:T(8,128)(2,1)} %param.22) | copy-start | bytes 3145732
  8.0 428.0 %all-reduce.2.cloned.1.call-start = ((), (), s32[]{:S(2)}) async-start(), calls=%async_computation.4 | async-start | bytes 4194304 | tf_op jit(solution)/shard_map/psum | solution.py:131
  10.1 1.3 collective-permute-start
  11.5 5.8 %collective-permute-start.1 = (bf16[2,128,256]{2,1,0:T(8,128)(2,1)S(1)}, bf16[2,128,256]{2,1,0:T(8,128)(2,1)S(1)}, u32[]{:S(2)}, u32[]{:S(2)}) collective-permute-start(bf16[2,128,256]{2,1,0:T(8,128)(2,1)S(1)} %pad_maximum_fusion.5), channel_id=1, source_target_pairs={{0,8},{4,12},{8,0},{12,4},{16,24},{20,28},{24,16},{28,20},{32,40},... | collective-permute-start | bytes 393224 | tf_op jit(solution)/shard_map/ppermute | solution.py:19
  17.4 15.0 %collective-permute-start.2 = (bf16[4,128,256]{2,1,0:T(8,128)(2,1)S(1)}, bf16[4,128,256]{2,1,0:T(8,128)(2,1)S(1)}, u32[]{:S(2)}, u32[]{:S(2)}) collective-permute-start(bf16[4,128,256]{2,1,0:T(8,128)(2,1)S(1)} %pad_maximum_fusion.4), channel_id=1, source_target_pairs={{0,16},{4,20},{8,24},{12,28},{16,0},{20,4},{24,8},{28,12},{32,48},... | collective-permute-start | bytes 786440 | tf_op jit(solution)/shard_map/ppermute | solution.py:19
  32.5 29.2 %collective-permute-start.3 = (bf16[8,128,256]{2,1,0:T(8,128)(2,1)S(1)}, bf16[8,128,256]{2,1,0:T(8,128)(2,1)S(1)}, u32[]{:S(2)}, u32[]{:S(2)}) collective-permute-start(bf16[8,128,256]{2,1,0:T(8,128)(2,1)S(1)} %pad_maximum_fusion.3), channel_id=1, source_target_pairs={{0,32},{4,36},{8,40},{12,44},{16,48},{20,52},{24,56},{28,60},{32,0... | collective-permute-start | bytes 1572872 | tf_op jit(solution)/shard_map/ppermute | solution.py:19
  61.8 0.8 copy-start.9
  61.8 1.0 copy-start.10
  62.8 24.1 %collective-permute-start.4 = (bf16[16,128,256]{2,1,0:T(8,128)(2,1)S(1)}, bf16[16,128,256]{2,1,0:T(8,128)(2,1)}, u32[]{:S(2)}, u32[]{:S(2)}) collective-permute-start(bf16[16,128,256]{2,1,0:T(8,128)(2,1)S(1)} %pad_maximum_fusion.2), channel_id=1, source_target_pairs={{0,64},{4,68},{8,72},{12,76},{16,80},{20,84},{24,88},{28,92},{32,9... | collective-permute-start | bytes 3145736 | tf_op jit(solution)/shard_map/ppermute | solution.py:19
  88.5 5.4 %copy-start.11 = (bf16[128,256]{1,0:T(8,128)(2,1)S(1)}, bf16[128,256]{1,0:T(8,128)(2,1)}, u32[]{:S(2)}) copy-start(bf16[128,256]{1,0:T(8,128)(2,1)} %param.23) | copy-start | bytes 196612
  88.5 17.7 %copy-start.16 = (s32[32]{0:T(128)S(1)}, s32[32]{0:T(128)}, u32[]{:S(2)}) copy-start(s32[32]{0:T(128)} %param.18) | copy-start | bytes 388
  88.5 17.8 %copy-start.13 = (s32[32]{0:T(128)S(1)}, s32[32]{0:T(128)}, u32[]{:S(2)}) copy-start(s32[32]{0:T(128)} %param.19) | copy-start | bytes 388
  88.5 17.8 %copy-start.14 = (bf16[500,8]{0,1:T(8,128)(2,1)S(1)}, bf16[500,8]{0,1:T(8,128)(2,1)}, u32[]{:S(2)}) copy-start(bf16[500,8]{0,1:T(8,128)(2,1)} %param.21) | copy-start | bytes 24004
  90.0 47.3 %collective-permute-start.5 = (bf16[32,128,256]{2,1,0:T(8,128)(2,1)}, bf16[32,128,256]{2,1,0:T(8,128)(2,1)}, u32[]{:S(2)}, u32[]{:S(2)}) collective-permute-start(bf16[32,128,256]{2,1,0:T(8,128)(2,1)} %pad_maximum_fusion.1), channel_id=1, source_target_pairs={{0,128},{4,132},{8,136},{12,140},{16,144},{20,148},{24,152},{28,15... | collective-permute-start | bytes 6291464 | tf_op jit(solution)/shard_map/ppermute | solution.py:19
  141.5 4.3 copy-start.4
  154.5 2.3 copy-start.12
  157.5 2.9 copy-start.2
  161.6 2.0 copy-start.3
  166.6 1.3 copy-start.6
  170.0 269.0 %reduce-scatter.3.cloned.1.call-start = ((), (), s32[]{:S(2)}) async-start(), calls=%async_computation.2 | async-start | bytes 655360 | tf_op jit(solution)/shard_map/reduce_scatter | solution.py:97
  171.7 1.6 copy-start.8
  173.3 1.6 copy-start.7
  176.5 264.1 %reduce-scatter.5.cloned.1.call-start = ((), (), s32[]{:S(2)}) async-start(), calls=%async_computation.3 | async-start | bytes 8519680 | tf_op jit(solution)/shard_map/reduce_scatter | solution.py:130
  176.5 4.3 copy-start.5
  281.1 161.5 %copy-start.1 = (bf16[8,256,256]{2,1,0:T(8,128)(2,1)S(1)}, bf16[8,256,256]{2,1,0:T(8,128)(2,1)}, u32[]{:S(2)}) copy-start(bf16[8,256,256]{2,1,0:T(8,128)(2,1)} %param.22) | copy-start | bytes 3145732
  281.7 158.9 %copy-start.15 = (s32[256]{0:T(256)S(1)}, s32[256]{0:T(256)}, u32[]{:S(2)}) copy-start(s32[256]{0:T(256)} %param.15) | copy-start | bytes 3076
Sparse Core Ops, SparseCore 0:
  170.2 265.7 all-reduce.1
Sparse Core Ops, SparseCore 1:
  176.6 22.9 reduce-scatter.2
  203.5 153.4 reduce-scatter.4
